TPU v7x, 128 devices: a whole 4x4x4 slice. The times are simulated.
128 devices in a mesh: dm: 2 (over core), bin: 64 (over x, y, z).
Axes of the slice: x: 4, y: 4, z: 4, core: 2. Of those that a mesh axis runs over, the one named last changes fastest.
Arguments:
- series: float32 [16777216], P(('dm', 'bin')), parts along dimension 0, may hold values from -6 to 6
- tap_coef: float32 [2, 16, 128], replicated, may hold values from -0.5 to 0.5
- tap_offset: int32 [16, 128], replicated, may hold values from 0 to 127, each once within a row
- harm_index: int32 [8, 524288], P(None, 'bin'), may hold values from 0 to 7, as said below
Outputs:
- summed: float32 [16, 1048576], P(None, ('dm', 'bin')), parts along dimension 1
There are 2 independent parts, one for each index of `dm`. A program takes and returns all parts, laid end to end along the dimension named above; an argument that names none is the same for every part. Nothing has to cross between parts.
Inputs may be any that keep to these rules, and one draw needn't show every extreme that they name: `harm_index`: entry (h, f) is at most h. `tap_offset`: each row holds every number below 128 once.
All inputs are finite; a program needn't handle non-finite values.
Results may differ from a plain program's by a relative error of at most 0.0014.
Values may be sent and summed in bfloat16 or wider, within the bound.
A program may use at most 256 MiB of HBM per device.

v0:
```python
import math

import jax
import jax.numpy as jnp
from jax import lax
from jax.sharding import PartitionSpec as P

DFT_LEN = 512
TMPL = 16
TAPS = 128
HARM = 8


PRECISE = lax.Precision.HIGHEST


def extended_2(cells, sides, width):
    for axis, dim in sides:
        count = lax.axis_size(axis)
        ends = count - 1
        head = lax.slice_in_dim(cells, 0, width, axis=dim)
        tail = lax.slice_in_dim(cells, cells.shape[dim] - width, cells.shape[dim], axis=dim)
        cells = jnp.concatenate(
            [
                lax.ppermute(tail, axis, [(i, (i + 1) % count) for i in range(ends)]),
                cells,
                lax.ppermute(head, axis, [((i + 1) % count, i) for i in range(ends)]),
            ],
            axis=dim,
        )
    return cells


def toeplitz_blocks(tap_coef, tap_offset):
    tap_count = tap_offset.shape[1]
    lag_index = jnp.arange(tap_count, dtype=jnp.int32)
    onehot = (tap_offset[:, :, None] == lag_index[None, None, :]).astype(jnp.float32)
    dense_taps = jnp.einsum("ztj,tjd->ztd", tap_coef, onehot, precision=PRECISE)
    window = jnp.arange(2 * tap_count, dtype=jnp.int32)
    banded = (window[None, None, :] - lag_index[None, :, None] == lag_index[:, None, None]).astype(
        jnp.float32
    )
    band_matrix = jnp.einsum("ztd,dim->ztim", dense_taps, banded, precision=PRECISE)
    real_rows = jnp.stack([band_matrix[0], -band_matrix[1]], axis=2)
    imag_rows = jnp.stack([band_matrix[1], band_matrix[0]], axis=2)
    return jnp.stack([real_rows, imag_rows], axis=1)


def granule_power(matrix, windows):
    result = jnp.einsum("toizm,zqm->toqi", matrix, windows, precision=PRECISE)
    return (result[:, 0] * result[:, 0] + result[:, 1] * result[:, 1]).astype(jnp.bfloat16)


def phase_table(first_index, second_index, modulus):
    product = first_index[:, None] * second_index[None, :] % modulus
    angle = product.astype(jnp.float32) * (2.0 * math.pi / modulus)
    return (jnp.cos(angle), -jnp.sin(angle))


def complex_apply(table_real, table_imag, operand, pattern):
    real_part = jnp.einsum(pattern, table_real, operand[0], precision=PRECISE) - jnp.einsum(
        pattern, table_imag, operand[1], precision=PRECISE
    )
    imag_part = jnp.einsum(pattern, table_real, operand[1], precision=PRECISE) + jnp.einsum(
        pattern, table_imag, operand[0], precision=PRECISE
    )
    return jnp.stack([real_part, imag_part])


def harmonic_plan(harmonic, position, devices, fund_count, granule):
    reach_count = (harmonic * fund_count + harmonic - 2) // granule + 2
    slot_depth = -(-reach_count // devices)
    requesters = jnp.arange(devices, dtype=jnp.int32)
    first_granule = harmonic * requesters * fund_count // granule
    first_slot = (first_granule - position + devices - 1) // devices
    return (slot_depth, first_slot)


def send_slots(extended, first_slot, slot_depth, devices):
    picks = first_slot[:, None] + jnp.arange(slot_depth, dtype=jnp.int32)[None, :]
    taken = jnp.take(extended, picks.reshape(-1), axis=1)
    return taken.reshape(extended.shape[0], devices, slot_depth, extended.shape[2])


def read_slots(
    received_flat,
    jitter_row,
    harmonic,
    position,
    devices,
    fund_count,
    granule,
    total_depth,
    slot_offset,
):
    fund_global = position * fund_count + jnp.arange(fund_count, dtype=jnp.int32)
    harm_row = harmonic * fund_global + jitter_row
    mine_first = harmonic * position * fund_count // granule
    target_granule = harm_row // granule
    owner = target_granule % devices
    owner_first = (mine_first - owner + devices - 1) // devices
    slot_index = target_granule // devices - owner_first
    flat_index = (owner * total_depth + slot_offset + slot_index) * granule + harm_row % granule
    return jnp.take(received_flat, flat_index, axis=1).astype(jnp.float32)


def owned_powers(contiguous, matrix, devices, granule):
    rim_width = granule // 2
    granule_count = contiguous.shape[1] // granule
    padded = extended_2(contiguous, (("bin", 1),), rim_width)
    pieces = padded.reshape(2, granule_count + 1, granule)
    windows = jnp.concatenate([pieces[:, :-1], pieces[:, 1:]], axis=2)
    local_power = granule_power(matrix, windows)
    spread = local_power.reshape(TMPL, granule_count // devices, devices, granule)
    cyclic = lax.all_to_all(spread, "bin", split_axis=2, concat_axis=1, tiled=True).reshape(
        TMPL, granule_count, granule
    )
    return cyclic


def shards(series, tap_coef, tap_offset, harm_index):
    devices = lax.axis_size("bin")
    position = lax.axis_index("bin")
    samples = series.shape[0]
    length = samples * devices
    dft_size = DFT_LEN
    outer_len = length // dft_size
    row_count = dft_size // devices
    col_count = outer_len // devices
    inner_len = outer_len // dft_size
    gathered = lax.all_to_all(
        series.reshape(row_count, outer_len), "bin", split_axis=1, concat_axis=0, tiled=True
    )
    freq_index = jnp.arange(dft_size, dtype=jnp.int32)
    cosine, sine = phase_table(freq_index, freq_index, dft_size)
    scale = 1.0 / math.sqrt(length)
    first_real = jnp.dot(cosine, gathered, precision=PRECISE) * scale
    first_imag = jnp.dot(sine, gathered, precision=PRECISE) * scale
    column_index = position * col_count + jnp.arange(col_count, dtype=jnp.int32)
    twist_real, twist_imag = phase_table(freq_index, column_index, length)
    turned = jnp.stack(
        [
            first_real * twist_real - first_imag * twist_imag,
            first_real * twist_imag + first_imag * twist_real,
        ]
    )
    regrouped = lax.all_to_all(turned, "bin", split_axis=1, concat_axis=2, tiled=True)
    grid = regrouped.reshape(2, row_count, inner_len, dft_size)
    small_index = jnp.arange(inner_len, dtype=jnp.int32)
    small_real, small_imag = phase_table(small_index, small_index, inner_len)
    section_one = complex_apply(small_real, small_imag, grid, "hg,cgb->chb")
    inner_real, inner_imag = phase_table(small_index, freq_index, outer_len)
    section_two = jnp.stack(
        [
            section_one[0] * inner_real - section_one[1] * inner_imag,
            section_one[0] * inner_imag + section_one[1] * inner_real,
        ]
    )
    spectral = complex_apply(cosine, sine, section_two, "be,chb->che")
    half_len = dft_size // 2
    per_dest = half_len // devices
    lower = spectral[:, :, :, :half_len].reshape(2, row_count, inner_len, devices, per_dest)
    outgoing = lower.transpose(0, 3, 4, 2, 1).reshape(2, devices, per_dest * inner_len * row_count)
    landed = lax.all_to_all(outgoing, "bin", split_axis=1, concat_axis=2, tiled=True)
    landed = landed.reshape(2, devices, per_dest, inner_len, row_count)
    contiguous = landed.transpose(0, 2, 3, 1, 4).reshape(2, per_dest * inner_len * dft_size)
    matrix = toeplitz_blocks(tap_coef, tap_offset)
    granule = TAPS
    fund_count = harm_index.shape[1]
    cyclic = owned_powers(contiguous, matrix, devices, granule)
    plans = [
        harmonic_plan(harmonic, position, devices, fund_count, granule)
        for harmonic in range(1, HARM + 1)
    ]
    deepest = max((plan_item[0] for plan_item in plans))
    extended = jnp.concatenate([cyclic, jnp.zeros((TMPL, deepest, granule), jnp.bfloat16)], axis=1)
    summed = jnp.zeros((TMPL, fund_count), jnp.float32)
    for harmonic in range(1, HARM + 1):
        slot_depth, first_slot = plans[harmonic - 1]
        outgoing_slots = send_slots(extended, first_slot, slot_depth, devices)
        received = lax.all_to_all(outgoing_slots, "bin", split_axis=1, concat_axis=1, tiled=True)
        received_flat = received.reshape(TMPL, devices * slot_depth * granule)
        summed = summed + read_slots(
            received_flat,
            harm_index[harmonic - 1],
            harmonic,
            position,
            devices,
            fund_count,
            granule,
            slot_depth,
            0,
        )
    return summed / HARM


def solution(mesh):
    return jax.shard_map(
        shards,
        mesh=mesh,
        in_specs=(P(("dm", "bin")), P(), P(), P(None, "bin")),
        out_specs=P(None, ("dm", "bin")),
        check_vma=False,
    )
```

profile of v0, /device:TPU:0, one launch (start us, length us, event | category | flops | bytes accessed | tf_op | source)
XLA Modules:
  0.0 699.3 jit_solution(5462952119762811340)
XLA Ops:
  2.3 11.5 %all-to-all-start = ((f32[8,64,256]{2,0,1:T(8,128)}), f32[8,64,256]{2,0,1:T(8,128)S(1)}, u32[]{:S(2)}, u32[]{:S(2)}) async-start(f32[8,64,256]{2,0,1:T(8,128)} %copy.70), calls=%async_computation | async-start | bytes 1048576 | tf_op jit(solution)/shard_map/all_to_all | solution.py:131
  13.8 13.1 %all-to-all-done = f32[8,64,256]{2,0,1:T(8,128)S(1)} async-done(((f32[8,64,256]{2,0,1:T(8,128)}), f32[8,64,256]{2,0,1:T(8,128)S(1)}, u32[]{:S(2)}, u32[]{:S(2)}) %all-to-all-start) | async-done | bytes 524320 | tf_op jit(solution)/shard_map/all_to_all | solution.py:131
  142.5 18.7 %fusion.8 = f32[16,2,512,128]{3,2,1,0:T(8,128)S(1)} fusion(f32[16,2,128,2,256]{4,0,2,3,1:T(8,128)} %pad_maximum_fusion, f32[2,512,128]{2,1,0:T(8,128)S(1)} %get-tuple-element.14, f32[2,512,128]{2,1,0:T(8,128)S(1)} %get-tuple-element.13), kind=kOutput, calls=%fused_computation.29 | convolution fusion | flops 12885164032 | bytes 17825792 | tf_op jit(solution)/shard_map/toizm,zqm->toqi/dot_general | solution.py:50
  164.5 9.1 %all-to-all-start.3 = ((bf16[16,8,64,128]{3,1,0,2:T(8,128)(2,1)}), bf16[16,8,64,128]{3,1,0,2:T(8,128)(2,1)S(1)}, u32[]{:S(2)}, u32[]{:S(2)}) async-start(bf16[16,8,64,128]{3,1,0,2:T(8,128)(2,1)} %copy.81), calls=%async_computation.3 | async-start | bytes 4194304 | tf_op jit(solution)/shard_map/all_to_all | solution.py:115
  174.3 26.9 %all-to-all-done.3 = bf16[16,8,64,128]{3,1,0,2:T(8,128)(2,1)S(1)} async-done(((bf16[16,8,64,128]{3,1,0,2:T(8,128)(2,1)}), bf16[16,8,64,128]{3,1,0,2:T(8,128)(2,1)S(1)}, u32[]{:S(2)}, u32[]{:S(2)}) %all-to-all-start.3) | async-done | bytes 2097184 | tf_op jit(solution)/shard_map/all_to_all | solution.py:115
  214.2 9.7 %all-to-all-done.4 = bf16[16,64,2,128]{3,0,2,1:T(8,128)(2,1)S(1)} async-done(((bf16[16,64,2,128]{3,0,2,1:T(8,128)(2,1)}), bf16[16,64,2,128]{3,0,2,1:T(8,128)(2,1)S(1)}, u32[]{:S(2)}, u32[]{:S(2)}) %all-to-all-start.4) | async-done | bytes 524320 | tf_op jit(solution)/shard_map/all_to_all | solution.py:181
  231.6 11.6 %all-to-all-done.5 = bf16[16,64,3,128]{3,0,2,1:T(8,128)(2,1)} async-done(((bf16[16,64,3,128]{3,0,2,1:T(8,128)(2,1)}), bf16[16,64,3,128]{3,0,2,1:T(8,128)(2,1)}, u32[]{:S(2)}, u32[]{:S(2)}) %all-to-all-start.5) | async-done | bytes 786464 | tf_op jit(solution)/shard_map/all_to_all | solution.py:181
  252.7 12.7 %all-to-all-done.6 = bf16[16,64,4,128]{3,0,2,1:T(8,128)(2,1)} async-done(((bf16[16,64,4,128]{3,0,2,1:T(8,128)(2,1)}), bf16[16,64,4,128]{3,0,2,1:T(8,128)(2,1)}, u32[]{:S(2)}, u32[]{:S(2)}) %all-to-all-start.6) | async-done | bytes 1048608 | tf_op jit(solution)/shard_map/all_to_all | solution.py:181
  275.4 15.4 %all-to-all-done.7 = bf16[16,64,5,128]{3,0,2,1:T(8,128)(2,1)S(1)} async-done(((bf16[16,64,5,128]{3,0,2,1:T(8,128)(2,1)}), bf16[16,64,5,128]{3,0,2,1:T(8,128)(2,1)S(1)}, u32[]{:S(2)}, u32[]{:S(2)}) %all-to-all-start.7) | async-done | bytes 1310752 | tf_op jit(solution)/shard_map/all_to_all | solution.py:181
  304.1 15.1 %all-to-all-done.8 = bf16[16,64,6,128]{3,0,2,1:T(8,128)(2,1)} async-done(((bf16[16,64,6,128]{3,0,2,1:T(8,128)(2,1)}), bf16[16,64,6,128]{3,0,2,1:T(8,128)(2,1)}, u32[]{:S(2)}, u32[]{:S(2)}) %all-to-all-start.8) | async-done | bytes 1572896 | tf_op jit(solution)/shard_map/all_to_all | solution.py:181
  339.4 11.6 %all-to-all-done.9 = bf16[16,64,7,128]{3,0,2,1:T(8,128)(2,1)} async-done(((bf16[16,64,7,128]{3,0,2,1:T(8,128)(2,1)}), bf16[16,64,7,128]{3,0,2,1:T(8,128)(2,1)}, u32[]{:S(2)}, u32[]{:S(2)}) %all-to-all-start.9) | async-done | bytes 1835040 | tf_op jit(solution)/shard_map/all_to_all | solution.py:181
  369.2 16.2 %all-to-all-done.10 = bf16[16,64,8,128]{3,0,2,1:T(8,128)(2,1)} async-done(((bf16[16,64,8,128]{3,0,2,1:T(8,128)(2,1)}), bf16[16,64,8,128]{3,0,2,1:T(8,128)(2,1)}, u32[]{:S(2)}, u32[]{:S(2)}) %all-to-all-start.10) | async-done | bytes 2097184 | tf_op jit(solution)/shard_map/all_to_all | solution.py:181
  397.7 24.6 %gather_fusion.1 = bf16[8192,16]{1,0:T(8,128)(2,1)S(1)} fusion(bf16[16,16384]{0,1:T(8,128)(2,1)} %bitcast.216, s32[8192]{0:T(1024)S(1)} %copy-done.12), kind=kCustom, calls=%fused_computation.1 | custom fusion | bytes 557056 | tf_op jit(solution)/shard_map/jit(_take)/gather | solution.py:104
  429.2 25.6 %gather_fusion.3 = bf16[8192,16]{1,0:T(8,128)(2,1)S(1)} fusion(bf16[16,24576]{0,1:T(8,128)(2,1)} %bitcast.215, s32[8192]{0:T(1024)S(1)} %copy-done.15), kind=kCustom, calls=%fused_computation.3 | custom fusion | bytes 557056 | tf_op jit(solution)/shard_map/jit(_take)/gather | solution.py:104
  463.2 26.5 %gather_fusion.5 = bf16[8192,16]{1,0:T(8,128)(2,1)S(1)} fusion(bf16[16,32768]{0,1:T(8,128)(2,1)} %bitcast.214, s32[8192]{0:T(1024)S(1)} %copy-done.14), kind=kCustom, calls=%fused_computation.5 | custom fusion | bytes 557056 | tf_op jit(solution)/shard_map/jit(_take)/gather | solution.py:104
  497.7 27.3 %gather_fusion.7 = bf16[8192,16]{1,0:T(8,128)(2,1)S(1)} fusion(bf16[16,40960]{0,1:T(8,128)(2,1)} %bitcast.213, s32[8192]{0:T(1024)S(1)} %copy-done.13), kind=kCustom, calls=%fused_computation.7 | custom fusion | bytes 557056 | tf_op jit(solution)/shard_map/jit(_take)/gather | solution.py:104
  525.8 9.9 %copy.101 = bf16[16,64,6,128]{0,3,2,1:T(8,128)(2,1)} copy(bf16[16,64,6,128]{3,0,2,1:T(8,128)(2,1)} %all-to-all-done.8) | data formatting | bytes 3145728 | tf_op jit(solution)/shard_map/all_to_all | solution.py:181
  535.7 28.1 %gather_fusion.9 = bf16[8192,16]{1,0:T(8,128)(2,1)S(1)} fusion(bf16[16,49152]{0,1:T(8,128)(2,1)} %bitcast.212, s32[8192]{0:T(1024)S(1)} %copy-done.11), kind=kCustom, calls=%fused_computation.9 | custom fusion | bytes 557056 | tf_op jit(solution)/shard_map/jit(_take)/gather | solution.py:104
  564.6 11.0 %copy.105 = bf16[16,64,7,128]{0,3,2,1:T(8,128)(2,1)} copy(bf16[16,64,7,128]{3,0,2,1:T(8,128)(2,1)} %all-to-all-done.9) | data formatting | bytes 3670016 | tf_op jit(solution)/shard_map/all_to_all | solution.py:181
  575.6 29.0 %gather_fusion.11 = bf16[8192,16]{1,0:T(8,128)(2,1)S(1)} fusion(bf16[16,57344]{0,1:T(8,128)(2,1)} %bitcast.211, s32[8192]{0:T(1024)S(1)} %broadcast_clamp_fusion.2), kind=kCustom, calls=%fused_computation.11 | custom fusion | bytes 557056 | tf_op jit(solution)/shard_map/jit(_take)/gather | solution.py:104
  606.0 12.4 %copy.109 = bf16[16,64,8,128]{0,3,2,1:T(8,128)(2,1)} copy(bf16[16,64,8,128]{3,0,2,1:T(8,128)(2,1)} %all-to-all-done.10) | data formatting | bytes 4194304 | tf_op jit(solution)/shard_map/all_to_all | solution.py:181
  618.4 29.9 %gather_fusion.13 = bf16[8192,16]{1,0:T(8,128)(2,1)S(1)} fusion(bf16[16,65536]{0,1:T(8,128)(2,1)} %bitcast.210, s32[8192]{0:T(1024)S(1)} %broadcast_clamp_fusion.1), kind=kCustom, calls=%fused_computation.13 | custom fusion | bytes 557056 | tf_op jit(solution)/shard_map/jit(_take)/gather | solution.py:104
  649.7 14.2 %copy.111 = bf16[16,64,9,128]{0,3,2,1:T(8,128)(2,1)} copy(bf16[16,64,9,128]{3,0,2,1:T(8,128)(2,1)} %all-to-all-done.11) | data formatting | bytes 4718592 | tf_op jit(solution)/shard_map/all_to_all | solution.py:181
  664.0 30.8 %gather_fusion.15 = bf16[8192,16]{1,0:T(8,128)(2,1)S(1)} fusion(bf16[16,73728]{0,1:T(8,128)(2,1)} %bitcast.209, s32[8192]{0:T(1024)S(1)} %broadcast_clamp_fusion), kind=kCustom, calls=%fused_computation.15 | custom fusion | bytes 557056 | tf_op jit(solution)/shard_map/jit(_take)/gather | solution.py:104
  (214 shorter events, 257.1 us)
Async XLA Ops:
  0.0 46.5 %copy-start = (f32[2,16,128]{2,1,0:T(8,128)S(1)}, f32[2,16,128]{2,1,0:T(8,128)}, u32[]{:S(2)}) copy-start(f32[2,16,128]{2,1,0:T(8,128)} %param.5) | copy-start | bytes 49156
  2.3 24.6 %all-to-all-start = ((f32[8,64,256]{2,0,1:T(8,128)}), f32[8,64,256]{2,0,1:T(8,128)S(1)}, u32[]{:S(2)}, u32[]{:S(2)}) async-start(f32[8,64,256]{2,0,1:T(8,128)} %copy.70), calls=%async_computation | async-start | bytes 1048576 | tf_op jit(solution)/shard_map/all_to_all | solution.py:131
  41.3 22.3 %all-to-all-start.1 = ((f32[2,512,256]{2,0,1:T(2,128)}), f32[2,512,256]{2,0,1:T(2,128)S(1)}, u32[]{:S(2)}, u32[]{:S(2)}) async-start(f32[2,512,256]{2,0,1:T(2,128)} %copy.71), calls=%async_computation.1 | async-start | bytes 2097152 | tf_op jit(solution)/shard_map/all_to_all | solution.py:147
  92.9 16.9 %all-to-all-start.2 = ((f32[2,64,1024]{2,0,1:T(2,128)}), f32[2,64,1024]{2,0,1:T(2,128)S(1)}, u32[]{:S(2)}, u32[]{:S(2)}) async-start(f32[2,64,1024]{2,0,1:T(2,128)} %copy.75), calls=%async_computation.2 | async-start | bytes 1048576 | tf_op jit(solution)/shard_map/all_to_all | solution.py:164
  122.7 19.1 %collective-permute-start.1 = (f32[2,64]{1,0:T(2,128)S(1)}, f32[2,64]{1,0:T(2,128)S(1)}, u32[]{:S(2)}, u32[]{:S(2)}) collective-permute-start(f32[2,64]{1,0:T(2,128)S(1)} %get-tuple-element.15), channel_id=1, source_target_pairs={{1,0},{2,1},{3,2},{4,3},{5,4},{6,5},{7,6},{8,7},{9,8},{10,9},{11,1... | collective-permute-start | bytes 1544 | tf_op jit(solution)/shard_map/ppermute | solution.py:27
  123.9 12.3 %collective-permute-start = (f32[2,64]{1,0:T(2,128)S(1)}, f32[2,64]{1,0:T(2,128)S(1)}, u32[]{:S(2)}, u32[]{:S(2)}) collective-permute-start(f32[2,64]{1,0:T(2,128)S(1)} %get-tuple-element.16), channel_id=1, source_target_pairs={{0,1},{1,2},{2,3},{3,4},{4,5},{5,6},{6,7},{7,8},{8,9},{9,10},{10,1... | collective-permute-start | bytes 1544 | tf_op jit(solution)/shard_map/ppermute | solution.py:25
  164.5 36.7 %all-to-all-start.3 = ((bf16[16,8,64,128]{3,1,0,2:T(8,128)(2,1)}), bf16[16,8,64,128]{3,1,0,2:T(8,128)(2,1)S(1)}, u32[]{:S(2)}, u32[]{:S(2)}) async-start(bf16[16,8,64,128]{3,1,0,2:T(8,128)(2,1)} %copy.81), calls=%async_computation.3 | async-start | bytes 4194304 | tf_op jit(solution)/shard_map/all_to_all | solution.py:115
  205.2 18.6 %all-to-all-start.4 = ((bf16[16,64,2,128]{3,0,2,1:T(8,128)(2,1)}), bf16[16,64,2,128]{3,0,2,1:T(8,128)(2,1)S(1)}, u32[]{:S(2)}, u32[]{:S(2)}) async-start(bf16[16,64,2,128]{3,0,2,1:T(8,128)(2,1)} %broadcast_select_fusion.7), calls=%async_computation.4 | async-start | bytes 1048576 | tf_op jit(solution)/shard_map/all_to_all | solution.py:181
  223.9 19.3 %all-to-all-start.5 = ((bf16[16,64,3,128]{3,0,2,1:T(8,128)(2,1)}), bf16[16,64,3,128]{3,0,2,1:T(8,128)(2,1)}, u32[]{:S(2)}, u32[]{:S(2)}) async-start(bf16[16,64,3,128]{3,0,2,1:T(8,128)(2,1)} %broadcast_select_fusion.6), calls=%async_computation.5 | async-start | bytes 1572864 | tf_op jit(solution)/shard_map/all_to_all | solution.py:181
  243.2 22.2 %all-to-all-start.6 = ((bf16[16,64,4,128]{3,0,2,1:T(8,128)(2,1)}), bf16[16,64,4,128]{3,0,2,1:T(8,128)(2,1)}, u32[]{:S(2)}, u32[]{:S(2)}) async-start(bf16[16,64,4,128]{3,0,2,1:T(8,128)(2,1)} %broadcast_select_fusion.5), calls=%async_computation.6 | async-start | bytes 2097152 | tf_op jit(solution)/shard_map/all_to_all | solution.py:181
  265.4 25.3 %all-to-all-start.7 = ((bf16[16,64,5,128]{3,0,2,1:T(8,128)(2,1)}), bf16[16,64,5,128]{3,0,2,1:T(8,128)(2,1)S(1)}, u32[]{:S(2)}, u32[]{:S(2)}) async-start(bf16[16,64,5,128]{3,0,2,1:T(8,128)(2,1)} %broadcast_select_fusion.4), calls=%async_computation.7 | async-start | bytes 2621440 | tf_op jit(solution)/shard_map/all_to_all | solution.py:181
  290.7 28.4 %all-to-all-start.8 = ((bf16[16,64,6,128]{3,0,2,1:T(8,128)(2,1)}), bf16[16,64,6,128]{3,0,2,1:T(8,128)(2,1)}, u32[]{:S(2)}, u32[]{:S(2)}) async-start(bf16[16,64,6,128]{3,0,2,1:T(8,128)(2,1)} %broadcast_select_fusion.3), calls=%async_computation.8 | async-start | bytes 3145728 | tf_op jit(solution)/shard_map/all_to_all | solution.py:181
  319.2 31.8 %all-to-all-start.9 = ((bf16[16,64,7,128]{3,0,2,1:T(8,128)(2,1)}), bf16[16,64,7,128]{3,0,2,1:T(8,128)(2,1)}, u32[]{:S(2)}, u32[]{:S(2)}) async-start(bf16[16,64,7,128]{3,0,2,1:T(8,128)(2,1)} %broadcast_select_fusion.2), calls=%async_computation.9 | async-start | bytes 3670016 | tf_op jit(solution)/shard_map/all_to_all | solution.py:181
  351.0 34.4 %all-to-all-start.10 = ((bf16[16,64,8,128]{3,0,2,1:T(8,128)(2,1)}), bf16[16,64,8,128]{3,0,2,1:T(8,128)(2,1)}, u32[]{:S(2)}, u32[]{:S(2)}) async-start(bf16[16,64,8,128]{3,0,2,1:T(8,128)(2,1)} %broadcast_select_fusion.1), calls=%async_computation.10 | async-start | bytes 4194304 | tf_op jit(solution)/shard_map/all_to_all | solution.py:181
  385.4 264.3 %all-to-all-start.11 = ((bf16[16,64,9,128]{3,0,2,1:T(8,128)(2,1)}), bf16[16,64,9,128]{3,0,2,1:T(8,128)(2,1)}, u32[]{:S(2)}, u32[]{:S(2)}) async-start(bf16[16,64,9,128]{3,0,2,1:T(8,128)(2,1)} %broadcast_select_fusion), calls=%async_computation.11 | async-start | bytes 4718592 | tf_op jit(solution)/shard_map/all_to_all | solution.py:181
  663.9 32.3 %copy-start.10 = (bf16[8192,16]{0,1:T(8,128)(2,1)S(1)}, bf16[8192,16]{0,1:T(8,128)(2,1)}, u32[]{:S(2)}) copy-start(bf16[8192,16]{0,1:T(8,128)(2,1)} %copy.94) | copy-start | bytes 786436
  663.9 32.3 %copy-start.17 = (pred[8192]{0:T(1024)(128)(4,1)S(1)}, pred[8192]{0:T(1024)(128)(4,1)}, u32[]{:S(2)}) copy-start(pred[8192]{0:T(1024)(128)(4,1)} %get-tuple-element.50) | copy-start | bytes 24580
  663.9 32.3 %copy-start.18 = (pred[8192]{0:T(1024)(128)(4,1)S(1)}, pred[8192]{0:T(1024)(128)(4,1)}, u32[]{:S(2)}) copy-start(pred[8192]{0:T(1024)(128)(4,1)} %get-tuple-element.45) | copy-start | bytes 24580
  663.9 32.3 %copy-start.19 = (pred[8192]{0:T(1024)(128)(4,1)S(1)}, pred[8192]{0:T(1024)(128)(4,1)}, u32[]{:S(2)}) copy-start(pred[8192]{0:T(1024)(128)(4,1)} %get-tuple-element.46) | copy-start | bytes 24580
  663.9 32.3 %copy-start.20 = (pred[8192]{0:T(1024)(128)(4,1)S(1)}, pred[8192]{0:T(1024)(128)(4,1)}, u32[]{:S(2)}) copy-start(pred[8192]{0:T(1024)(128)(4,1)} %get-tuple-element.47) | copy-start | bytes 24580
  663.9 32.3 %copy-start.21 = (pred[8192]{0:T(1024)(128)(4,1)S(1)}, pred[8192]{0:T(1024)(128)(4,1)}, u32[]{:S(2)}) copy-start(pred[8192]{0:T(1024)(128)(4,1)} %get-tuple-element.48) | copy-start | bytes 24580
  664.0 32.3 %copy-start.22 = (pred[8192]{0:T(1024)(128)(4,1)S(1)}, pred[8192]{0:T(1024)(128)(4,1)}, u32[]{:S(2)}) copy-start(pred[8192]{0:T(1024)(128)(4,1)} %get-tuple-element.43) | copy-start | bytes 24580
  664.0 32.3 %copy-start.23 = (pred[8192]{0:T(1024)(128)(4,1)S(1)}, pred[8192]{0:T(1024)(128)(4,1)}, u32[]{:S(2)}) copy-start(pred[8192]{0:T(1024)(128)(4,1)} %get-tuple-element.44) | copy-start | bytes 24580
  664.0 34.9 %copy-start.1 = (f32[2,16,128]{2,1,0:T(8,128)S(1)}, f32[2,16,128]{2,1,0:T(8,128)}, u32[]{:S(2)}) copy-start(f32[2,16,128]{2,1,0:T(8,128)} %param.5) | copy-start | bytes 49156
  (15 other events, 167.0 us)
where the time goes:
time: 711 us; the launch traced here: 699 us
  local copies, waits for them, and re-layouts  357 us (50%)
  waiting for transfers between devices  143 us (20%)
  starting transfers between devices  80.8 us (11%)
  matrix products  62.6 us (9%)
  other arithmetic  53.5 us (8%)
    gather x16, local copies, waits for them, and re-layouts, read_slots(): return jnp.take(received_flat, flat_index, axis=1).astype(jnp.float32)  232 us
    all_to_all x8, waiting for transfers between devices, shards(): lax.all_to_all(outgoing_slots, 'bin', split_axis=1, concat_axis=1, tiled=...  92.2 us
    all_to_all x8, local copies, waits for them, and re-layouts, shards(): lax.all_to_all(outgoing_slots, 'bin', split_axis=1, concat_axis=1, tiled=...  69.5 us
    all_to_all x8, starting transfers between devices, shards(): lax.all_to_all(outgoing_slots, 'bin', split_axis=1, concat_axis=1, tiled=...  44.8 us
    all_to_all x1, waiting for transfers between devices, owned_powers(): lax.all_to_all(spread, 'bin', split_axis=2, concat_axis=1, tiled=True)  26.9 us
    dot_general x1, matrix products, granule_power(): result = jnp.einsum('toizm,zqm->toqi', matrix, windows, precision=PRECISE)  18.7 us
    select_n x16, other arithmetic, send_slots(): taken = jnp.take(extended, picks.reshape(-1), axis=1)  16.2 us
    gather x8, local copies, waits for them, and re-layouts, send_slots(): taken = jnp.take(extended, picks.reshape(-1), axis=1)  15.6 us
  transfers between devices with their start and end apart: 14, of which 11 were waited for; matrix products, arithmetic and copies ran while one was open for 48% of the time, Pallas kernels for 0%

commit v1 on v0

v1 whole, which is shorter than its diff:
```python
import functools
import math

import jax
import jax.numpy as jnp
import numpy as np
from jax import lax
from jax.experimental import pallas as pl
from jax.experimental.pallas import tpu as pltpu
from jax.sharding import PartitionSpec as P

D = 64
TMPL = 16
TAPS = 128
HARM = 8
LENGTH = 8388608
LOCAL = LENGTH // D
ALPHA = 512
BETA = 256
ORDER = (8, 7, 1, 6, 2, 5, 3, 4)
BLOCKS = tuple((h, r) for h in ORDER for r in range(h))
NB = len(BLOCKS)
FIRST = {h: BLOCKS.index((h, 0)) for h in ORDER}
ROWS = 80
HALO = 72
F32 = jnp.float32
BF16 = jnp.bfloat16


def np_split(x):
    x = np.asarray(x, np.float32)
    hi = x.astype(jnp.bfloat16)
    lo = (x - hi.astype(np.float32)).astype(jnp.bfloat16)
    return hi, lo


@functools.lru_cache(None)
def fft_tables():
    k1 = np.arange(D)[:, None]
    m = np.arange(LOCAL // D)[None, :]
    ang = -2 * np.pi * (k1 * m) / LENGTH
    tw1 = np.stack([np.cos(ang), np.sin(ang)]).astype(np.float32)
    k = np.arange(ALPHA)[:, None] * np.arange(ALPHA)[None, :] % ALPHA
    ang = -2 * np.pi * k / ALPHA
    c, s = np.cos(ang), np.sin(ang)
    wa = np.block([[c, -s], [s, c]])
    ang = -2 * np.pi * (np.arange(ALPHA)[:, None] * np.arange(BETA)[None, :]) / LOCAL
    tw2 = np.stack([np.cos(ang), np.sin(ang)]).astype(np.float32)
    half = BETA // 2
    ang = -2 * np.pi * (np.arange(BETA)[:, None] * np.arange(half)[None, :] % BETA) / BETA
    c, s = np.cos(ang), np.sin(ang)
    vb = np.block([[c, s], [-s, c]])
    return tw1, *np_split(wa), tw2, *np_split(vb)


@functools.lru_cache(None)
def perm_tables():
    out = []
    for h in range(1, HARM + 1):
        m = np.zeros((128 * h, 128 * h), np.float32)
        a = np.arange(128)
        for r in range(h):
            m[h * a + r, 128 * r + a] = 1
        out.append(m.astype(jnp.bfloat16))
    return tuple(out)


@functools.lru_cache(None)
def select_tables():
    i = np.arange(64)
    e = np.zeros((NB, 128, 128), np.float32)
    ex = np.zeros((NB, 64, 128), np.float32)
    jp = np.zeros((NB, 1, 128), np.float32)
    for n, (h, r) in enumerate(BLOCKS):
        b, j = np.divmod(64 * r + i, h)
        for t in range(2):
            e[n, 64 * t + i, 64 * t + b] = 1
            ex[n, b, 64 * t + i] = 1
            jp[n, 0, 64 * t + i] = j
    return e.astype(jnp.bfloat16), ex.astype(jnp.bfloat16), jp


def split(x):
    hi = x.astype(BF16)
    return hi, (x - hi.astype(F32)).astype(BF16)


def dot(a, b):
    return jnp.dot(a, b, preferred_element_type=F32)


def dot3(ah, al, bh, bl):
    return dot(ah, bh) + dot(ah, bl) + dot(al, bh)


def columns_kernel(xs, w1, tw, out):
    x = jnp.concatenate([xs[pl.ds(m, D, stride=16), :] for m in range(16)], axis=1)
    y = dot3(*split(w1[...]), *split(x))
    yr, yi = y[:D], y[D:]
    zr = yr * tw[0] - yi * tw[1]
    zi = yr * tw[1] + yi * tw[0]
    for c, z in enumerate((zr, zi)):
        for m in range(16):
            out[pl.ds(c * 16 + (m % 2) * 8 + m // 2, D, stride=32), :] = z[:, 128 * m : 128 * m + 128]


def local_fft_kernel(b, wah, wal, tw, vbh, vbl, *rest):
    perms, out, zn = rest[:HARM], rest[HARM], rest[HARM + 1]
    v = b[...].reshape(D, 4, 8, 128)
    parts = [v[:, n].reshape(ALPHA, 128) for n in range(4)]
    rhs = jnp.concatenate(
        [jnp.concatenate(parts[0:2], axis=1), jnp.concatenate(parts[2:4], axis=1)], axis=0
    )
    y = dot3(wah[...], wal[...], *split(rhs))
    yr, yi = y[:ALPHA], y[ALPHA:]
    t = jnp.concatenate([yr * tw[0] - yi * tw[1], yr * tw[1] + yi * tw[0]], axis=1)
    th, tl = split(t)
    z = dot3(th, tl, vbh[...], vbl[...])
    zero = jnp.zeros((8, 128), F32)
    for c in range(2):
        zt = z[:, 128 * c : 128 * c + 128].T
        zn[c, 0:8, :] = zero
        zn[c, 520:528, :] = zero
        for n in range(4):
            zn[c, pl.ds(8 + n, 128, stride=4), :] = zt[:, 128 * n : 128 * n + 128]
    lane = lax.broadcasted_iota(jnp.int32, (D, 128), 1)
    halo = jnp.zeros((D, 128), F32)
    for h in range(1, HARM + 1):
        src = jnp.concatenate(
            [
                jnp.concatenate([zn[c, pl.ds(8 + n, D, stride=h), :] for n in range(h)], axis=1)
                for c in range(2)
            ],
            axis=0,
        )
        hi, lo = split(src)
        moved = dot(jnp.concatenate([hi, lo], axis=0), perms[h - 1][...])
        moved = moved[:128] + moved[128:]
        for r in range(h):
            for c in range(2):
                out[pl.ds(2 * (FIRST[h] + r) + c, D, stride=ROWS), :] = moved[
                    64 * c : 64 * c + 64, 128 * r : 128 * r + 128
                ]
        for c in range(2):
            left = zn[c, pl.ds(7, D, stride=h), :][:, 127:128]
            right = zn[c, pl.ds(8 + h, D, stride=h), :][:, 0:1]
            halo = jnp.where(lane == c * 8 + h - 1, left, halo)
            halo = jnp.where(lane == 16 + c * 8 + h - 1, right, halo)
    out[pl.ds(HALO, D, stride=ROWS), :] = halo
    for n in range(HALO + 1, ROWS):
        out[pl.ds(n, D, stride=ROWS), :] = jnp.zeros((D, 128), F32)


def search_kernel(land, jit, taps, e, ex, jp, out, xt, xl, pm, msk, sm):
    lane8 = lax.broadcasted_iota(jnp.int32, (8, 128), 1)
    for n in range(NB):
        re = land[pl.ds(2 * n, D, stride=ROWS), :]
        im = land[pl.ds(2 * n + 1, D, stride=ROWS), :]
        xt[n, 8:136, :] = jnp.concatenate([re, im], axis=0).T
    edge = land[pl.ds(HALO, D, stride=ROWS), :]
    et = jnp.concatenate([edge, jnp.zeros((D, 128), F32)], axis=0).T
    left = jnp.where(lane8 < 64, et[0:8], pltpu.roll(et[8:16], 64, 1))
    right = jnp.where(lane8 < 64, et[16:24], pltpu.roll(et[24:32], 64, 1))
    for h in range(1, HARM + 1):
        xt[FIRST[h] + h - 1, 7:8, :] = left[h - 1 : h]
        xt[FIRST[h], 136:137, :] = right[h - 1 : h]

    def put(n, slot, hi, lo):
        xl[pl.ds(128 * n, 128), pl.ds(128 * slot, 128)] = hi
        xl[pl.ds(128 * n, 128), pl.ds(384 + 128 * slot, 128)] = lo

    for n, (h, r) in enumerate(BLOCKS):
        hi, lo = split(xt[n, 8:136, :])
        put(n, 1, hi, lo)
        if r > 0:
            put(n - 1, 2, hi, lo)
        if r < h - 1:
            put(n + 1, 0, hi, lo)
        if r == 0:
            put(n, 0, *split(xt[n + h - 1, 7:135, :]))
        if r == h - 1:
            put(n, 2, *split(xt[n - h + 1, 9:137, :]))
        msk[pl.ds(128 * n, 128), :] = jnp.where(dot(jit[h - 1], ex[n]) == jp[n], 1.0, 0.0)

    def template_pair(tp, carry):
        for g in range(NB // 4):
            rows = pl.ds(512 * g, 512)
            lhs = jnp.concatenate([xl[rows, :], xl[rows, 0:384]], axis=1)
            acc = dot(lhs, taps[tp])
            re, im = acc[:, :128], acc[:, 128:]
            kept = jnp.where(msk[rows, :] > 0.5, re * re + im * im, 0.0).astype(BF16)
            for q in range(4):
                pm[4 * g + q, pl.ds(pl.multiple_of(128 * tp, 128), 128), :] = kept[128 * q : 128 * q + 128]
        return carry

    lax.fori_loop(0, TMPL // 2, template_pair, 0)
    lane = lax.broadcasted_iota(jnp.int32, (64, 128), 1)

    def finish(tp, carry):
        rows = pl.ds(pl.multiple_of(256 * tp, 256), 256)
        total = jnp.zeros((256, 128), F32)
        for n in range(0, NB, 2):
            total += dot(
                jnp.concatenate([pm[n, rows, :], pm[n + 1, rows, :]], axis=1),
                jnp.concatenate([e[n], e[n + 1]], axis=0),
            )
        sm[...] = total * (1.0 / HARM)
        for q in range(2):
            even = sm[pl.ds(128 * q, 64, stride=2), :]
            odd = sm[pl.ds(128 * q + 1, 64, stride=2), :]
            out[4 * tp + 2 * q] = jnp.where(lane < 64, even, pltpu.roll(odd, 64, 1))
            out[4 * tp + 2 * q + 1] = jnp.where(lane < 64, pltpu.roll(even, 64, 1), odd)
        return carry

    lax.fori_loop(0, TMPL // 4, finish, 0)


def vmem(count):
    return [pl.BlockSpec(memory_space=pltpu.VMEM)] * count


def call(kernel, count, shape, scratch=(), flops=0, moved=0, limit=56):
    return pl.pallas_call(
        kernel,
        out_shape=jax.ShapeDtypeStruct(shape, F32),
        in_specs=vmem(count),
        out_specs=pl.BlockSpec(memory_space=pltpu.VMEM),
        scratch_shapes=list(scratch),
        compiler_params=pltpu.CompilerParams(vmem_limit_bytes=limit * 1024 * 1024),
        cost_estimate=pl.CostEstimate(flops=flops, bytes_accessed=moved, transcendentals=0),
    )


def columns(xs, w1, tw1):
    return call(columns_kernel, 3, (2048, 128), flops=10**8, moved=3 * 10**6)(xs, w1, tw1)


def local_fft(b, wah, wal, tw2, vbh, vbl, perms):
    return call(
        local_fft_kernel,
        6 + HARM,
        (D * ROWS, 128),
        [pltpu.VMEM((2, 528, 128), F32)],
        flops=4 * 10**9,
        moved=2 * 10**7,
    )(b, wah, wal, tw2, vbh, vbl, *perms)


def search(land, jit, taps, e, ex, jp):
    return call(
        search_kernel,
        6,
        (TMPL, 64, 128),
        [
            pltpu.VMEM((NB, 144, 128), F32),
            pltpu.VMEM((NB * 128, 768), BF16),
            pltpu.VMEM((NB, 1024, 128), BF16),
            pltpu.VMEM((NB * 128, 128), F32),
            pltpu.VMEM((256, 128), F32),
        ],
        flops=25 * 10**9,
        moved=2 * 10**7,
    )(land, jit, taps, e, ex, jp)


def device_matrix(e):
    k1 = jnp.arange(D, dtype=jnp.int32)[:, None]
    n1 = jnp.arange(D, dtype=jnp.int32)[None, :]
    ang = (k1 * (D * n1 + e) % (D * D)).astype(F32) * (2 * math.pi / (D * D))
    scale = 1.0 / math.sqrt(LENGTH)
    return jnp.concatenate([jnp.cos(ang), -jnp.sin(ang)], axis=0) * scale


def tap_matrix(tap_coef, tap_offset):
    lag = jnp.arange(TAPS, dtype=jnp.int32)
    onehot = (tap_offset[:, :, None] == lag[None, None, :]).astype(F32)
    dense = jnp.einsum("ztj,tjd->ztd", tap_coef, onehot, precision=lax.Precision.HIGHEST)
    parts = jnp.stack([jnp.stack([dense[0], dense[1]]), jnp.stack([-dense[1], dense[0]])])
    w = jnp.arange(192, dtype=jnp.int32)
    i = jnp.arange(64, dtype=jnp.int32)
    band = (w[None, :, None] - i[None, None, :] == lag[:, None, None]).astype(BF16)
    hi = lax.reduce_precision(parts, 8, 7)
    both = jnp.stack([hi, parts - hi]).astype(BF16)
    full = jnp.einsum("scotd,dwi->scotwi", both, band, preferred_element_type=F32).astype(BF16)
    full = full.reshape(2, 2, 2, TMPL // 2, 2, 3, 64, 64)
    full = full.transpose(3, 0, 5, 1, 6, 2, 4, 7).reshape(TMPL // 2, 2, 384, 256)
    return jnp.concatenate([full[:, 0], full[:, 0], full[:, 1]], axis=1)


def shards(series, tap_coef, tap_offset, harm_index):
    e = lax.axis_index("bin")
    tw1, wah, wal, tw2, vbh, vbl = fft_tables()
    xs = lax.all_to_all(series.reshape(D, 16, 128), "bin", split_axis=0, concat_axis=0, tiled=True)
    part = columns(xs.reshape(1024, 128), device_matrix(e), tw1)
    got = lax.all_to_all(part.reshape(D, 32, 128), "bin", split_axis=0, concat_axis=0, tiled=True)
    send = local_fft(got.reshape(2048, 128), wah, wal, tw2, vbh, vbl, perm_tables())
    land = lax.all_to_all(send.reshape(D, ROWS, 128), "bin", split_axis=0, concat_axis=0, tiled=True)
    jit = harm_index.reshape(HARM, 128, 64).astype(BF16)
    out = search(land.reshape(D * ROWS, 128), jit, tap_matrix(tap_coef, tap_offset), *select_tables())
    return out.reshape(TMPL, 8192)


def solution(mesh):
    return jax.shard_map(
        shards,
        mesh=mesh,
        in_specs=(P(("dm", "bin")), P(), P(), P(None, "bin")),
        out_specs=P(None, ("dm", "bin")),
        check_vma=False,
    )
```

time: 711 us -> 153 us (0.22); the launches traced: 699 us -> 152 us
  local copies, waits for them, and re-layouts: 357 us -> 36.8 us
  waiting for transfers between devices: 143 us -> 12.3 us
  starting transfers between devices: 80.8 us -> 17.5 us
  matrix products: 62.6 us -> 6.47 us
  Pallas kernels: 0 us -> 53.4 us
  other arithmetic: 53.5 us -> 3.15 us
  blocking collectives: 0 us -> 22.5 us
    gather x24 -> x0, local copies, waits for them, and re-layouts: 248 us -> none  [the longest x16 232 us: read_slots(): return jnp.take(received_flat, flat_index, axis=1).astype(jnp.float32)]
    all_to_all x12 -> x2, waiting for transfers between devices: 143 us -> 12.3 us  [the longest x1 12.3 us: shards(): lax.all_to_all(series.reshape(D, 16, 128), 'bin', split_axis=0, concat_ax...]
    all_to_all x13 -> x0, local copies, waits for them, and re-layouts: 73.3 us -> none  [the longest x8 69.5 us: shards(): lax.all_to_all(outgoing_slots, 'bin', split_axis=1, concat_axis=1, tiled=...]
    all_to_all x12 -> x2, starting transfers between devices: 74.9 us -> 17.5 us  [the longest x1 11.6 us: shards(): lax.all_to_all(series.reshape(D, 16, 128), 'bin', split_axis=0, concat_ax...]
    dot_general x13 -> x2, matrix products: 62.6 us -> 6.47 us  [the longest x1 5.75 us: tap_matrix(): jnp.einsum('scotd,dwi->scotwi', both, band, preferred_element_type=F32)]
    pallas_call x0 -> x3, Pallas kernels: none -> 53.4 us  [the longest x1 35.4 us: search(): call(search_kernel, 6, (TMPL, 64, 128), [pltpu.VMEM((NB, 144, 128), F32),...]
    select_n x21 -> x0, other arithmetic: 24.4 us -> none  [the longest x16 16.2 us: send_slots(): taken = jnp.take(extended, picks.reshape(-1), axis=1)]
    all_to_all x0 -> x1, blocking collectives: none -> 22.5 us  [shards(): lax.all_to_all(part.reshape(D, 32, 128), 'bin', split_axis=0, concat_axis...]
  transfers between devices with their start and end apart: 14 -> 2, of which waited for: 11 -> 1; matrix products, arithmetic and copies ran while one was open for 48% -> 29% of each run, Pallas kernels for 0% -> 0%
where the time goes in v1:
time: 153 us; the launch traced here: 152 us
  Pallas kernels  53.4 us (35%)
  local copies, waits for them, and re-layouts  36.8 us (24%)
  blocking collectives  22.5 us (15%)
  starting transfers between devices  17.5 us (11%)
  waiting for transfers between devices  12.3 us (8%)
  matrix products  6.47 us (4%)
  other arithmetic  3.15 us (2%)
    pallas_call x1, Pallas kernels, search(): call(search_kernel, 6, (TMPL, 64, 128), [pltpu.VMEM((NB, 144, 128), F32),...  35.4 us
    all_to_all x1, blocking collectives, shards(): lax.all_to_all(part.reshape(D, 32, 128), 'bin', split_axis=0, concat_axis...  22.5 us
    pallas_call x1, Pallas kernels, local_fft(): call(local_fft_kernel, 6 + HARM, (D * ROWS, 128), [pltpu.VMEM((2, 528, 12...  14.4 us
    transpose x1, local copies, waits for them, and re-layouts, tap_matrix(): full.transpose(3, 0, 5, 1, 6, 2, 4, 7).reshape(TMPL // 2, 2, 384, 256)  12.7 us
    all_to_all x1, waiting for transfers between devices, shards(): lax.all_to_all(series.reshape(D, 16, 128), 'bin', split_axis=0, concat_ax...  12.3 us
    all_to_all x1, starting transfers between devices, shards(): lax.all_to_all(series.reshape(D, 16, 128), 'bin', split_axis=0, concat_ax...  11.6 us
    reshape x1, local copies, waits for them, and re-layouts, tap_matrix(): full.transpose(3, 0, 5, 1, 6, 2, 4, 7).reshape(TMPL // 2, 2, 384, 256)  11 us
    convert_element_type x1, local copies, waits for them, and re-layouts, tap_matrix(): jnp.einsum('scotd,dwi->scotwi', both, band, preferred_element_type=F32)  8.91 us
  transfers between devices with their start and end apart: 2, of which 1 were waited for; matrix products, arithmetic and copies ran while one was open for 29% of the time, Pallas kernels for 0%

profile of v1, /device:TPU:0, one launch (start us, length us, event | category | flops | bytes accessed | tf_op | source)
XLA Modules:
  0.0 152.2 jit_solution(700474372558051739)
XLA Ops:
  0.0 0.0 copy-start
  0.0 11.6 %all-to-all-start = ((f32[64,16,128]{2,1,0:T(8,128)}), f32[64,16,128]{2,1,0:T(8,128)S(1)}, u32[]{:S(2)}, u32[]{:S(2)}) async-start(f32[64,16,128]{2,1,0:T(8,128)} %bitcast.44), calls=%async_computation | async-start | bytes 1048576 | tf_op jit(solution)/shard_map/all_to_all | solution.py:293
  11.7 0.2 fusion.19
  11.8 0.6 maximum_multiply_fusion.w1
  12.4 12.3 %all-to-all-done = f32[64,16,128]{2,1,0:T(8,128)S(1)} async-done(((f32[64,16,128]{2,1,0:T(8,128)}), f32[64,16,128]{2,1,0:T(8,128)S(1)}, u32[]{:S(2)}, u32[]{:S(2)}) %all-to-all-start) | async-done | bytes 524320 | tf_op jit(solution)/shard_map/all_to_all | solution.py:293
  24.7 0.8 copy-done.1
  25.5 3.6 %shard_map.199 = f32[2048,128]{1,0:T(8,128)} custom-call(f32[1024,128]{1,0:T(8,128)} %bitcast.43, f32[128,64]{1,0:T(8,128)} %maximum_multiply_fusion.w1, f32[2,64,2048]{2,1,0:T(8,128)} %constant.59.clone.tw), custom_call_target="tpu_custom_call" | custom-call | flops 100000000 | bytes 3000000 | tf_op jit(solution)/shard_map/pallas_call | solution.py:235
  29.1 22.5 %all_to_all.15 = f32[64,32,128]{2,1,0:T(8,128)} all-to-all(f32[64,32,128]{2,1,0:T(8,128)} %bitcast.41), channel_id=1, replica_groups=mesh['dm'=2,'bin'=64] {'bin'}, dimensions={0} | all-to-all | bytes 2097152 | tf_op jit(solution)/shard_map/all_to_all | solution.py:295
  51.6 14.4 %shard_map.200 = f32[5120,128]{1,0:T(8,128)} custom-call(f32[2048,128]{1,0:T(8,128)} %bitcast.42, bf16[1024,1024]{1,0:T(8,128)(2,1)} %constant.60.clone.wah, bf16[1024,1024]{1,0:T(8,128)(2,1)} %constant.61.clone.wal, f32[2,512,256]{2,1,0:T(8,128)} %constant.62.clone.tw, bf16[512,256]{1,0:T(8,128)(2,1)} %constant.63.clone.vbh, ...), custom_call_target="tpu_custom_call" | custom-call | flops 4000000000 | bytes 20000000 | tf_op jit(solution)/shard_map/pallas_call | solution.py:239
  66.0 5.9 %all-to-all-start.2 = ((f32[64,80,128]{2,1,0:T(8,128)}), f32[64,80,128]{2,1,0:T(8,128)}, u32[]{:S(2)}, u32[]{:S(2)}) async-start(f32[64,80,128]{2,1,0:T(8,128)} %bitcast.40), calls=%async_computation.2 | async-start | bytes 5242880 | tf_op jit(solution)/shard_map/all_to_all | solution.py:297
  71.9 0.0 copy-done
  71.9 0.0 copy-done.3
  71.9 0.7 fusion.7
  72.7 5.8 %fusion.4 = bf16[2,2,2,16,192,64]{4,3,5,2,1,0:T(8,128)(2,1)} fusion(s32[192,64]{0,1:T(8,128)S(1)} %iota_subtract_fusion, bf16[1,2,2,16,128]{4,3,2,1,0:T(8,128)(2,1)S(1)} %get-tuple-element.8, bf16[1,2,2,16,128]{4,3,2,1,0:T(8,128)(2,1)S(1)} %get-tuple-element.7), kind=kOutput, calls=%fused_computation.5 | convolution fusion | flops 405864448 | bytes 3227648 | tf_op jit(solution)/shard_map/scotd,dwi->scotwi/dot_general | solution.py:284
  78.4 8.9 %copy.31 = bf16[2,2,2,16,192,64]{5,4,3,2,1,0:T(8,128)(2,1)} copy(bf16[2,2,2,16,192,64]{4,3,5,2,1,0:T(8,128)(2,1)} %fusion.4) | data formatting | bytes 6291456 | tf_op jit(solution)/shard_map/convert_element_type | solution.py:284
  87.3 12.7 %copy.32 = bf16[8,2,3,2,64,2,2,64]{7,6,5,4,3,2,0,1:T(2,128)(2,1)} copy(bf16[8,2,3,2,64,2,2,64]{7,4,2,6,0,5,3,1:T(8,128)(2,1)} %bitcast.39) | data formatting | bytes 6291456 | tf_op jit(solution)/shard_map/transpose | solution.py:286
  100.1 11.0 %reshape.133 = bf16[8,2,384,256]{3,2,0,1:T(8,128)(2,1)S(1)} reshape(bf16[8,2,3,2,64,2,2,64]{7,6,5,4,3,2,0,1:T(2,128)(2,1)} %copy.32) | data formatting | bytes 6291456 | tf_op jit(solution)/shard_map/reshape | solution.py:286
  111.1 0.0 copy-done.2
  111.1 1.0 convert_element_type.16.jit
  112.1 0.2 slice_bitcast_fusion.1
  112.3 2.3 %pad_maximum_fusion.taps = bf16[8,1152,256]{2,1,0:T(8,128)(2,1)} fusion(bf16[8,384,256]{2,1,0:T(8,128)(2,1)S(1)} %get-tuple-element.6, bf16[8,384,256]{2,1,0:T(8,128)(2,1)S(1)} %get-tuple-element.5), kind=kLoop, calls=%fused_computation.3 | loop fusion | flops 14155776 | bytes 7864320 | tf_op jit(solution)/shard_map/concatenate | solution.py:287
  114.6 0.0 all-to-all-done.2
  114.6 35.4 %shard_map.201 = f32[16,64,128]{2,1,0:T(8,128)} custom-call(f32[5120,128]{1,0:T(8,128)} %bitcast.5.land, bf16[8,128,64]{2,1,0:T(8,128)(2,1)} %convert_element_type.16.jit, bf16[8,1152,256]{2,1,0:T(8,128)(2,1)} %pad_maximum_fusion.taps, bf16[36,128,128]{2,1,0:T(8,128)(2,1)} %constant.73.clone.e, bf16[36,64,128]{2,1,0:T(8,128)(2,1)} %constant.74.clone.ex, ...), custom_call_target="tpu_custom_call" | custom-call | flops 24999999488 | bytes 20000000 | tf_op jit(solution)/shard_map/pallas_call | solution.py:250
  150.0 2.1 %copy.41 = f32[2,8,64,128]{3,1,2,0:T(8,128)} copy(f32[2,8,64,128]{3,2,1,0:T(8,128)} %bitcast.45) | data formatting | bytes 1048576
  (10 shorter events, 0.1 us)
Async XLA Ops:
  0.0 71.9 %copy-start = (f32[2,16,128]{2,1,0:T(8,128)S(1)}, f32[2,16,128]{2,1,0:T(8,128)}, u32[]{:S(2)}) copy-start(f32[2,16,128]{2,1,0:T(8,128)} %param.22) | copy-start | bytes 49156
  0.0 24.7 %all-to-all-start = ((f32[64,16,128]{2,1,0:T(8,128)}), f32[64,16,128]{2,1,0:T(8,128)S(1)}, u32[]{:S(2)}, u32[]{:S(2)}) async-start(f32[64,16,128]{2,1,0:T(8,128)} %bitcast.44), calls=%async_computation | async-start | bytes 1048576 | tf_op jit(solution)/shard_map/all_to_all | solution.py:293
  24.7 0.8 copy-start.1
  66.0 5.9 %copy-start.3 = (s32[16,128]{1,0:T(8,128)S(1)}, s32[16,128]{1,0:T(8,128)}, u32[]{:S(2)}) copy-start(s32[16,128]{1,0:T(8,128)} %param.23) | copy-start | bytes 24580
  66.0 48.6 %all-to-all-start.2 = ((f32[64,80,128]{2,1,0:T(8,128)}), f32[64,80,128]{2,1,0:T(8,128)}, u32[]{:S(2)}, u32[]{:S(2)}) async-start(f32[64,80,128]{2,1,0:T(8,128)} %bitcast.40), calls=%async_computation.2 | async-start | bytes 5242880 | tf_op jit(solution)/shard_map/all_to_all | solution.py:297
  100.1 11.0 %copy-start.2 = (s32[8,8192]{1,0:T(8,128)S(1)}, s32[8,8192]{1,0:T(8,128)}, u32[]{:S(2)}) copy-start(s32[8,8192]{1,0:T(8,128)} %param.24) | copy-start | bytes 786436
